TPU v7x, 32 devices: a whole 2x2x4 slice. The times are simulated.
32 devices in a mesh: dp: 16 (over z, y, core), expert: 2 (over x).
Axes of the slice: x: 2, y: 2, z: 4, core: 2. Of those that a mesh axis runs over, the one named last changes fastest.
Arguments:
- activations: bfloat16 [1024, 4096], P('expert', 'dp'), may hold values from -6 to 6
- out_grad: bfloat16 [1024, 4096], P('expert', 'dp'), may hold values from -6 to 6
- w_in: bfloat16 [2, 4096, 8192], P('expert', None, 'dp'), may hold values from -0.125 to 0.125
- w_out: bfloat16 [2, 8192, 4096], P('expert', 'dp'), may hold values from -0.0625 to 0.0625
- chosen: int32 [2, 256], replicated, may hold values from 0 to 1023, as said below
- gate_scores: float32 [2, 256], P('expert'), may hold values from 0.2 to 1
Outputs:
- w_in_grad: bfloat16 [2, 4096, 8192], P('expert', None, 'dp')
- w_out_grad: bfloat16 [2, 8192, 4096], P('expert', 'dp')
- act_grad: bfloat16 [1024, 4096], P('expert', 'dp')
- gate_grad: float32 [2, 256], P('expert')
Inputs may be any that keep to these rules, and one draw needn't show every extreme that they name: Each row of chosen holds 256 distinct token numbers.
All inputs are finite; a program needn't handle non-finite values.
Results may differ from a plain program's by a relative error of at most 0.0075.
Values may be sent and summed in bfloat16 or wider, within the bound.
A program may use at most 64 MiB of HBM per device.

v0:
```python
import jax
import jax.numpy as jnp
from jax import lax
from jax.sharding import PartitionSpec as P

GELU_SCALE = 0.7978845608
CUBIC_COEF = 0.044715


def gelu_parts(preact):
    inner = GELU_SCALE * (preact + CUBIC_COEF * preact * preact * preact)
    tanh_part = jnp.tanh(inner)
    gelu_val = 0.5 * preact * (1.0 + tanh_part)
    gelu_slope = 0.5 * (1.0 + tanh_part) + 0.5 * preact * (
        1.0 - tanh_part * tanh_part
    ) * GELU_SCALE * (1.0 + 3.0 * CUBIC_COEF * preact * preact)
    return (gelu_val, gelu_slope)


def contract(left_operand, right_operand, left_axis, right_axis):
    return lax.dot_general(
        left_operand,
        right_operand,
        (((left_axis,), (right_axis,)), ((), ())),
        preferred_element_type=jnp.float32,
    )


def exact_contract(left_operand, right_operand, left_axis, right_axis):
    return lax.dot_general(
        left_operand,
        right_operand,
        (((left_axis,), (right_axis,)), ((), ())),
        precision=lax.Precision.HIGHEST,
        preferred_element_type=jnp.float32,
    )


def input_sum(weight_in, preact_back):
    return lax.psum_scatter(
        contract(weight_in, preact_back, 1, 1), "dp", scatter_dimension=0, tiled=True
    )


def per_device(activations, out_grad, w_in, w_out, chosen, gate_scores):
    expert_id = lax.axis_index("expert")
    experts = lax.axis_size("expert")
    own_rows = activations.shape[0]
    every_act, every_grad = (
        lax.all_gather(activations, "expert", axis=0, tiled=True),
        lax.all_gather(out_grad, "expert", axis=0, tiled=True),
    )
    picked = lax.dynamic_index_in_dim(chosen, expert_id, 0, keepdims=False)
    inputs, upstream = (
        lax.all_gather(jnp.take(every_act, picked, axis=0), "dp", axis=1, tiled=True),
        lax.all_gather(jnp.take(every_grad, picked, axis=0), "dp", axis=1, tiled=True),
    )
    weight_in = w_in[0]
    weight_out = w_out[0]
    scores = gate_scores[0]
    gated_grad = (scores[:, None] * upstream.astype(jnp.float32)).astype(jnp.bfloat16)
    preact = jnp.dot(inputs, weight_in, preferred_element_type=jnp.float32)
    gelu_val, gelu_slope = gelu_parts(preact)
    hidden = gelu_val.astype(jnp.bfloat16)
    raw_back = contract(upstream, weight_out, 1, 1)
    gate_grad = lax.psum(jnp.sum(hidden.astype(jnp.float32) * raw_back, axis=1), "dp")
    hidden_back = contract(gated_grad, weight_out, 1, 1)
    preact_back = (hidden_back * gelu_slope).astype(jnp.bfloat16)
    weight_in_grad = contract(inputs, preact_back, 0, 0).astype(jnp.bfloat16)
    weight_out_grad = contract(hidden, gated_grad, 0, 0).astype(jnp.bfloat16)
    summed = input_sum(weight_in, preact_back)
    accumulated = jnp.zeros((summed.shape[0], own_rows), jnp.float32)
    expert_terms = lax.all_gather(summed[None], "expert", axis=0, tiled=True)
    token_ids = expert_id * own_rows + lax.iota(jnp.int32, own_rows)
    for expert_num in range(experts):
        onehot = (chosen[expert_num][None, :] == token_ids[:, None]).astype(jnp.float32)
        accumulated = accumulated + exact_contract(expert_terms[expert_num], onehot, 1, 1)
    act_grad = accumulated.T.astype(jnp.bfloat16)
    return (weight_in_grad[None], weight_out_grad[None], act_grad, gate_grad[None])


def solution(mesh):
    return jax.shard_map(
        per_device,
        mesh=mesh,
        in_specs=(
            P("expert", "dp"),
            P("expert", "dp"),
            P("expert", None, "dp"),
            P("expert", "dp", None),
            P(),
            P("expert", None),
        ),
        out_specs=(
            P("expert", None, "dp"),
            P("expert", "dp", None),
            P("expert", "dp"),
            P("expert", None),
        ),
        check_vma=False,
    )
```

profile of v0, /device:TPU:0, one launch (start us, length us, event | category | flops | bytes accessed | tf_op | source)
XLA Modules:
  0.0 209.8 jit_solution(7828869161212420655)
XLA Ops:
  7.2 0.0 all-gather.4.cloned.1.call-start
  7.2 0.8 fusion.36
  8.1 10.2 %all_gather.15 = bf16[1024,256]{1,0:T(8,128)(2,1)S(1)} all-gather(bf16[512,256]{1,0:T(8,128)(2,1)} %param.8), channel_id=1, replica_groups=mesh['dp'=16,'expert'=2] {'expert'}, dimensions={0}, use_global_device_ids=true | all-gather | bytes 786432 | tf_op jit(solution)/shard_map/all_gather | solution.py:50
  18.2 8.4 %all_gather.17 = bf16[1024,256]{1,0:T(8,128)(2,1)S(1)} all-gather(bf16[512,256]{1,0:T(8,128)(2,1)} %param.9), channel_id=1, replica_groups=mesh['dp'=16,'expert'=2] {'expert'}, dimensions={0}, use_global_device_ids=true | all-gather | bytes 786432 | tf_op jit(solution)/shard_map/all_gather | solution.py:51
  26.6 1.2 gather_fusion
  27.7 1.2 gather_fusion.1
  28.9 0.0 copy-start.3
  28.9 0.8 broadcast_select_fusion
  29.7 0.0 all-gather.4.cloned.1.call-update
  29.7 0.0 all-gather.6.cloned.1.call-start
  29.8 0.7 all-gather.6.cloned.1.call-update
  30.5 0.0 reduce-scatter.2.cloned.1.call-start
  30.5 41.7 %all-gather.4.cloned.1.call-done = bf16[256,4096]{1,0:T(8,128)(2,1)} async-done(((bf16[256,256]{1,0:T(8,128)(2,1)}), bf16[256,4096]{1,0:T(8,128)(2,1)}) %all-gather.4.cloned.1.call-update) | async-done | bytes 2097168 | tf_op jit(solution)/shard_map/all_gather | solution.py:55
  72.2 4.1 %fusion.3 = f32[256,512]{1,0:T(8,128)S(1)} fusion(bf16[256,4096]{1,0:T(8,128)(2,1)} %all-gather.4.cloned.1.call-done, bf16[1,4096,512]{2,1,0:T(8,128)(2,1)} %param.10), kind=kOutput, calls=%fused_computation.8 | convolution fusion | flops 1073741824 | bytes 6815744 | tf_op jit(solution)/shard_map/dot_general | solution.py:62
  76.3 38.8 %all-gather.6.cloned.1.call-done = bf16[256,4096]{1,0:T(8,128)(2,1)} async-done(((bf16[256,256]{1,0:T(8,128)(2,1)}), bf16[256,4096]{1,0:T(8,128)(2,1)}) %all-gather.6.cloned.1.call-update) | async-done | bytes 2097168 | tf_op jit(solution)/shard_map/all_gather | solution.py:56
  115.1 0.0 copy-done.3
  115.1 0.0 copy-start.1
  115.1 4.5 %fusion.15 = bf16[256,512]{1,0:T(8,128)(2,1)S(1)} fusion(bf16[1,512,4096]{2,1,0:T(8,128)(2,1)} %param.11, bf16[256,4096]{1,0:T(8,128)(2,1)} %all-gather.6.cloned.1.call-done, f32[256]{0:T(256)S(1)} %bitcast.38, f32[256,512]{1,0:T(8,128)S(1)} %fusion.3), kind=kOutput, calls=%fused_computation.18 | convolution fusion | flops 1079377920 | bytes 7078912 | tf_op jit(solution)/shard_map/dot_general | solution.py:21
  119.6 0.0 copy-done.1
  119.6 3.2 %convolution_bitcast_fusion = f32[4096,256]{0,1:T(8,128)} fusion(bf16[256,512]{1,0:T(8,128)(2,1)S(1)} %fusion.15, bf16[1,4096,512]{2,1,0:T(8,128)(2,1)S(1)} %copy-done.1), kind=kOutput, calls=%fused_computation.6 | convolution fusion | flops 1073741824 | bytes 8650752 | tf_op jit(solution)/shard_map/dot_general | solution.py:21
  122.8 0.0 reduce-scatter.2.cloned.1.call-update
  122.9 0.0 copy-start
  122.9 4.4 %fusion.19 = f32[256]{0:T(256)S(1)} fusion(bf16[256,4096]{1,0:T(8,128)(2,1)} %all-gather.6.cloned.1.call-done, bf16[1,512,4096]{2,1,0:T(8,128)(2,1)} %param.11, f32[256,512]{1,0:T(8,128)S(1)} %fusion.3), kind=kOutput, calls=%fused_computation.20 | convolution fusion | flops 1075314432 | bytes 6816768 | tf_op jit(solution)/shard_map/dot_general | solution.py:21
  127.2 32.5 %psum.7 = f32[1,256]{1,0:T(1,128)} all-reduce(f32[1,256]{1,0:T(1,128)S(1)} %bitcast.40), channel_id=1, replica_groups=mesh['dp'=16,'expert'=2] {'dp'}, use_global_device_ids=true, to_apply=%region_2.4 | all-reduce | flops 256 | bytes 2048 | tf_op jit(solution)/shard_map/psum | solution.py:66
  159.7 0.0 copy-done
  159.7 0.0 copy-start.2
  159.7 3.3 %fusion = bf16[1,4096,512]{2,1,0:T(8,128)(2,1)} fusion(bf16[256,4096]{1,0:T(8,128)(2,1)S(1)} %copy-done, bf16[256,512]{1,0:T(8,128)(2,1)S(1)} %fusion.15), kind=kOutput, calls=%fused_computation.4 | convolution fusion | flops 1075838976 | bytes 6553600 | tf_op jit(solution)/shard_map/dot_general | solution.py:21
  163.0 0.0 copy-done.2
  163.0 3.5 %fusion.1 = bf16[1,512,4096]{2,1,0:T(8,128)(2,1)} fusion(bf16[256,4096]{1,0:T(8,128)(2,1)S(1)} %copy-done.2, f32[256]{0:T(256)S(1)} %bitcast.39, f32[256,512]{1,0:T(8,128)S(1)} %fusion.3), kind=kOutput, calls=%fused_computation.5 | convolution fusion | flops 1080164352 | bytes 6816768 | tf_op jit(solution)/shard_map/dot_general | solution.py:21
  166.6 27.9 %reduce-scatter.2.cloned.1.call-done = f32[256,256]{0,1:T(8,128)} async-done(((f32[4096,256]{0,1:T(8,128)}), f32[256,256]{0,1:T(8,128)}) %reduce-scatter.2.cloned.1.call-update) | async-done | bytes 262160 | tf_op jit(solution)/shard_map/reduce_scatter | solution.py:40
  194.4 7.2 %all-gather = f32[512,256]{0,1:T(8,128)S(1)} all-gather(f32[256,256]{0,1:T(8,128)} %reduce-scatter.2.cloned.1.call-done), channel_id=2, replica_groups=mesh['dp'=16,'expert'=2] {'expert'}, dimensions={0}, use_global_device_ids=true | all-gather | bytes 786432 | tf_op jit(solution)/shard_map/all_gather | solution.py:73
  201.7 0.4 fusion.28
  202.1 1.1 fusion.18
  (4 shorter events, 0.0 us)
Async XLA Ops:
  7.2 65.1 %all-gather.4.cloned.1.call-start = ((), (), s32[]{:S(2)}) async-start(), calls=%async_computation.1 | async-start | bytes 2228224 | tf_op jit(solution)/shard_map/all_gather | solution.py:55
  28.9 86.2 %copy-start.3 = (f32[1,256]{1,0:T(1,128)S(1)}, f32[1,256]{1,0:T(1,128)}, u32[]{:S(2)}) copy-start(f32[1,256]{1,0:T(1,128)} %param.13) | copy-start | bytes 3076
  29.7 85.4 %all-gather.6.cloned.1.call-start = ((), (), s32[]{:S(2)}) async-start(), calls=%async_computation.2 | async-start | bytes 2228224 | tf_op jit(solution)/shard_map/all_gather | solution.py:56
  30.5 164.0 %reduce-scatter.2.cloned.1.call-start = ((), (), s32[]{:S(2)}) async-start(), calls=%async_computation.3 | async-start | bytes 4456448 | tf_op jit(solution)/shard_map/reduce_scatter | solution.py:40
  115.1 4.5 %copy-start.1 = (bf16[1,4096,512]{2,1,0:T(8,128)(2,1)S(1)}, bf16[1,4096,512]{2,1,0:T(8,128)(2,1)}, u32[]{:S(2)}) copy-start(bf16[1,4096,512]{2,1,0:T(8,128)(2,1)} %param.10) | copy-start | bytes 12582916
  122.9 36.9 %copy-start = (bf16[256,4096]{1,0:T(8,128)(2,1)S(1)}, bf16[256,4096]{1,0:T(8,128)(2,1)}, u32[]{:S(2)}) copy-start(bf16[256,4096]{1,0:T(8,128)(2,1)} %all-gather.4.cloned.1.call-done) | copy-start | bytes 6291460
  159.7 3.3 %copy-start.2 = (bf16[256,4096]{1,0:T(8,128)(2,1)S(1)}, bf16[256,4096]{1,0:T(8,128)(2,1)}, u32[]{:S(2)}) copy-start(bf16[256,4096]{1,0:T(8,128)(2,1)} %all-gather.6.cloned.1.call-done) | copy-start | bytes 6291460
Sparse Core Ops, SparseCore 0:
  29.9 42.3 all-gather.3
  75.0 40.1 all-gather.5
  123.0 71.4 reduce-scatter.1
where the time goes:
time: 210 us
  waiting for transfers between devices  109 us (52%)
  blocking collectives  58.3 us (28%)
  matrix products  24.5 us (12%)
  between operations  13.8 us (7%)
  local copies, waits for them, and re-layouts  3.12 us (1%)
    all_gather x1, waiting for transfers between devices, per_device(): lax.all_gather(jnp.take(every_act, picked, axis=0), 'dp', axis=1, tiled=T...  41.7 us
    all_gather x1, waiting for transfers between devices, per_device(): lax.all_gather(jnp.take(every_grad, picked, axis=0), 'dp', axis=1, tiled=...  38.8 us
    psum x1, blocking collectives, per_device(): lax.psum(jnp.sum(hidden.astype(jnp.float32) * raw_back, axis=1), 'dp')  32.5 us
    reduce_scatter x1, waiting for transfers between devices, input_sum(): lax.psum_scatter(contract(weight_in, preact_back, 1, 1), 'dp', scatter_di...  27.9 us
    dot_general x5, matrix products, contract(): lax.dot_general(left_operand, right_operand, (((left_axis,), (right_axis,...  18.9 us
    all_gather x1, blocking collectives, per_device(): lax.all_gather(activations, 'expert', axis=0, tiled=True)  10.2 us
    all_gather x1, blocking collectives, per_device(): lax.all_gather(out_grad, 'expert', axis=0, tiled=True)  8.37 us
    all_gather x1, blocking collectives, per_device(): expert_terms = lax.all_gather(summed[None], 'expert', axis=0, tiled=True)  7.25 us
  transfers between devices with their start and end apart: 3, of which 3 were waited for; matrix products, arithmetic and copies ran while one was open for 7% of the time, Pallas kernels for 0%

commit v1 on v0

--- a/solution.py
+++ b/solution.py
@@ -1,6 +1,8 @@
 import jax
 import jax.numpy as jnp
 from jax import lax
+from jax.experimental import pallas as pl
+from jax.experimental.pallas import tpu as pltpu
 from jax.sharding import PartitionSpec as P
 
 GELU_SCALE = 0.7978845608
@@ -78,24 +80,365 @@
     act_grad = accumulated.T.astype(jnp.bfloat16)
     return (weight_in_grad[None], weight_out_grad[None], act_grad, gate_grad[None])
 
+def flip(bit, with_bit):
+    return bit + with_bit - 2 * bit * with_bit
+
+
+def fused_kernel(
+    act_ref, grad_ref, win_hbm, wout_hbm, chosen_ref, scores_ref,
+    wing_hbm, woutg_hbm, actg_ref, gate_ref,
+    win_v, wout_v, wing_v, woutg_v, gat, xsend, xrecv, pre, raw,
+    hidden_t, back_b, gate_rows, part, s_send, s_recv, q_keep, y_send, y_recv,
+    z_send, z_recv, t_send, t_recv, g_send, g_recv, local_sem, send_sem, recv_sem,
+):
+    me = lax.axis_index("dp")
+    expert = lax.axis_index("expert")
+    other = 1 - expert
+    bits = [me % 2, (me // 2) % 2, (me // 4) % 2, (me // 8) % 2]
+    own_rows, width = act_ref.shape
+    rows = chosen_ref.shape[1]
+    hidden_units = win_v.shape[1]
+    zgroups = 4
+    group_width = 4 * width
+
+    def peer(mask):
+        index = 0
+        for place in range(4):
+            bit = bits[place]
+            index = index + (1 - bit if (mask >> place) & 1 else bit) * (1 << place)
+        return {"dp": index}
+
+    x_peer = {"expert": other}
+
+    def group_of(kz):
+        low = 1 - bits[2] if kz & 1 else bits[2]
+        high = 1 - bits[3] if kz & 2 else bits[3]
+        return low + 2 * high
+
+    loads = [
+        pltpu.make_async_copy(win_hbm.at[0], win_v, local_sem.at[0]),
+        pltpu.make_async_copy(wout_hbm.at[0], wout_v, local_sem.at[1]),
+    ]
+    for load in loads:
+        load.start()
+
+    barrier = pltpu.get_barrier_semaphore()
+    targets = [peer(1), peer(2), peer(4), peer(8), peer(12), x_peer]
+    for target in targets:
+        pl.semaphore_signal(
+            barrier, inc=1, device_id=target, device_id_type=pl.DeviceIdType.MESH
+        )
+
+    token = expert * own_rows + lax.broadcasted_iota(jnp.int32, (own_rows, rows), 0)
+
+    def onehot(which):
+        picked = chosen_ref[pl.ds(which, 1), :]
+        return jnp.where(picked == token, 1.0, 0.0).astype(jnp.bfloat16)
+
+    own_hot = onehot(expert)
+    other_hot = onehot(other)
+
+    ids = {}
+
+    def slot_of(key):
+        return ids.setdefault(key, len(ids))
+
+    started = []
+    incoming = {}
+
+    def send(source, landing, target, key):
+        number = slot_of(key)
+        copy = pltpu.make_async_remote_copy(
+            src_ref=source,
+            dst_ref=landing,
+            send_sem=send_sem.at[number],
+            recv_sem=recv_sem.at[number],
+            device_id=target,
+            device_id_type=pl.DeviceIdType.MESH,
+        )
+        copy.start()
+        started.append(copy)
+        incoming[key] = copy
+
+    xsend[0] = contract(other_hot, act_ref[...], 0, 0).astype(jnp.bfloat16)
+    pl.semaphore_wait(barrier, len(targets))
+    send(xsend.at[0], xrecv.at[0], x_peer, ("x", 0))
+    xsend[1] = contract(other_hot, grad_ref[...], 0, 0).astype(jnp.bfloat16)
+    send(xsend.at[1], xrecv.at[1], x_peer, ("x", 1))
+    own_picks = [
+        contract(own_hot, ref[...], 0, 0).astype(jnp.bfloat16)
+        for ref in (act_ref, grad_ref)
+    ]
+    pre[...] = jnp.zeros_like(pre)
+    raw[...] = jnp.zeros_like(raw)
+
+    def pass_on(array, k, mask):
+        send(gat.at[array, k], gat.at[array, k ^ mask], peer(mask), ("g", array, k ^ mask))
+
+    def arrived(array, k):
+        incoming[("g", array, k)].wait_recv()
+
+    def add_group(kz):
+        base = group_of(kz)
+
+        def body(step, carry):
+            lane = flip(bits[0], step % 2) + 2 * flip(bits[1], step // 2)
+            start = pl.multiple_of((4 * base + lane) * width, width)
+            slot = 4 * kz + step
+            pre[...] += jnp.dot(
+                gat[0, slot], win_v[pl.ds(start, width), :],
+                preferred_element_type=jnp.float32,
+            )
+            raw[...] += contract(gat[1, slot], wout_v[:, pl.ds(start, width)], 1, 1)
+            return carry
+
+        lax.fori_loop(0, 4, body, 0)
+
+    for array in range(2):
+        incoming[("x", array)].wait_recv()
+        gat[array, 0] = own_picks[array] + xrecv[array]
+        for mask in (4, 2, 8, 12, 1):
+            pass_on(array, 0, mask)
+    for load in loads:
+        load.wait()
+    for step in range(1, zgroups + 2):
+        for array in range(2):
+            if step < zgroups:
+                arrived(array, 4 * step)
+                pass_on(array, 4 * step, 2)
+                pass_on(array, 4 * step, 1)
+        for array in range(2):
+            if step <= zgroups:
+                arrived(array, 4 * (step - 1) + 2)
+                pass_on(array, 4 * (step - 1) + 2, 1)
+        if step >= 2:
+            for array in range(2):
+                arrived(array, 4 * (step - 2) + 1)
+                arrived(array, 4 * (step - 2) + 3)
+            add_group(step - 2)
+
+    chunk = 32
+    score_col = jnp.broadcast_to(scores_ref[...], (128, rows)).T
+    gate_rows[...] = score_col
+
+    def activate(step, carry):
+        span = pl.ds(pl.multiple_of(step * chunk, chunk), chunk)
+        gelu_val, gelu_slope = gelu_parts(pre[span, :])
+        back = raw[span, :]
+        score = jnp.concatenate([gate_rows[span, :]] * (hidden_units // 128), axis=1)
+        hidden = gelu_val.astype(jnp.bfloat16).astype(jnp.float32)
+        product = hidden * back
+        folded = product[:, :128]
+        for piece in range(1, hidden_units // 128):
+            folded = folded + product[:, piece * 128:(piece + 1) * 128]
+        back_b[span, :] = (score * back * gelu_slope).astype(jnp.bfloat16)
+        pre[span, :] = score * gelu_val
+        gate_rows[span, :] = folded
+        return carry
+
+    lax.fori_loop(0, rows // chunk, activate, 0)
+
+    def partials(kz):
+        base = group_of(kz)
+
+        def body(step, carry):
+            lane = flip(bits[0], step % 2) + 2 * flip(bits[1], step // 2)
+            start = pl.multiple_of((4 * base + lane) * width, width)
+            part[4 * kz + step] = contract(
+                back_b[...], win_v[pl.ds(start, width), :], 1, 1
+            )
+            return carry
+
+        lax.fori_loop(0, 4, body, 0)
+        for ky in range(2):
+            place = 2 * kz + ky
+            s_send[place] = part[4 * kz + 2 * ky + 1].astype(jnp.bfloat16)
+            send(s_send.at[place], s_recv.at[place], peer(1), ("s", place))
+
+    def pair_sums(kz):
+        place = 2 * kz + 1
+        incoming[("s", place)].wait_recv()
+        y_send[kz] = (part[4 * kz + 2] + s_recv[place].astype(jnp.float32)).astype(
+            jnp.bfloat16
+        )
+        send(y_send.at[kz], y_recv.at[kz], peer(2), ("y", kz))
+        incoming[("s", place - 1)].wait_recv()
+        q_keep[kz] = part[4 * kz] + s_recv[place - 1].astype(jnp.float32)
+
+    order = (2, 3, 1, 0)
+    for position, kz in enumerate(order):
+        partials(kz)
+        if position:
+            pair_sums(order[position - 1])
+    pair_sums(order[-1])
+
+    g_send[0] = jnp.broadcast_to(
+        jnp.sum(gate_rows[...].T, axis=0, keepdims=True), (8, rows)
+    )
+    send(g_send.at[0], g_recv.at[0], peer(1), ("gate", 0))
+    hidden_t[...] = pre[...].T.astype(jnp.bfloat16)
+
+    stores = []
+
+    def weight_grads(kz):
+        base = group_of(kz)
+
+        def body(step, carry):
+            lane = flip(bits[0], step % 2) + 2 * flip(bits[1], step // 2)
+            start = pl.multiple_of((4 * base + lane) * width, width)
+            slot = 4 * kz + step
+            wing_v[pl.ds(start, width), :] = contract(
+                gat[0, slot], back_b[...], 0, 0
+            ).astype(jnp.bfloat16)
+            woutg_v[:, pl.ds(start, width)] = jnp.dot(
+                hidden_t[...], gat[1, slot], preferred_element_type=jnp.float32
+            ).astype(jnp.bfloat16)
+            return carry
+
+        lax.fori_loop(0, 4, body, 0)
+        span = pl.ds(pl.multiple_of(base * group_width, group_width), group_width)
+        for copy in (
+            pltpu.make_async_copy(
+                wing_v.at[span, :], wing_hbm.at[0, span, :], local_sem.at[2 + 2 * kz]
+            ),
+            pltpu.make_async_copy(
+                woutg_v.at[:, span], woutg_hbm.at[0, :, span], local_sem.at[3 + 2 * kz]
+            ),
+        ):
+            copy.start()
+            stores.append(copy)
+
+    weight_grads(0)
+    incoming[("gate", 0)].wait_recv()
+    g_send[1] = g_send[0] + g_recv[0]
+    send(g_send.at[1], g_recv.at[1], peer(2), ("gate", 1))
+
+    total = None
+    for kz in order:
+        incoming[("y", kz)].wait_recv()
+        value = q_keep[kz] + y_recv[kz].astype(jnp.float32)
+        if kz:
+            z_send[kz - 1] = value.astype(jnp.bfloat16)
+            send(z_send.at[kz - 1], z_recv.at[kz - 1], peer(4 * kz), ("z", kz - 1))
+            if kz == order[0]:
+                incoming[("gate", 1)].wait_recv()
+                g_send[2] = g_send[1] + g_recv[1]
+                for kg in range(1, zgroups):
+                    send(g_send.at[2], g_recv.at[1 + kg], peer(4 * kg), ("gate", 1 + kg))
+            weight_grads(kz)
+        else:
+            q_keep[0] = value
+    total = q_keep[0]
+    for kz in order[:-1]:
+        incoming[("z", kz - 1)].wait_recv()
+        total = total + z_recv[kz - 1].astype(jnp.float32)
+    t_send[...] = total.astype(jnp.bfloat16)
+    send(t_send, t_recv, x_peer, ("t", 0))
+    for kg in range(1, zgroups):
+        incoming[("gate", 1 + kg)].wait_recv()
+    gate_sum = (g_send[2] + g_recv[2]) + (g_recv[3] + g_recv[4])
+    gate_ref[...] = gate_sum[0:1, :]
+    mine = jnp.dot(own_hot, t_send[...], preferred_element_type=jnp.float32)
+    incoming[("t", 0)].wait_recv()
+    theirs = jnp.dot(other_hot, t_recv[...], preferred_element_type=jnp.float32)
+    actg_ref[...] = (mine + theirs).astype(jnp.bfloat16)
+    for copy in stores:
+        copy.wait()
+    for copy in started:
+        copy.wait_send()
+
+
+def fused(activations, out_grad, w_in, w_out, chosen, gate_scores):
+    own_rows, width = activations.shape
+    _, model, hidden_units = w_in.shape
+    rows = chosen.shape[1]
+    copies = 64
+    half, full = jnp.bfloat16, jnp.float32
+    vmem = pl.BlockSpec(memory_space=pltpu.VMEM)
+    anywhere = pl.BlockSpec(memory_space=pl.ANY)
+    return pl.pallas_call(
+        fused_kernel,
+        out_shape=(
+            jax.ShapeDtypeStruct((1, model, hidden_units), half),
+            jax.ShapeDtypeStruct((1, hidden_units, model), half),
+            jax.ShapeDtypeStruct((own_rows, width), half),
+            jax.ShapeDtypeStruct((1, rows), full),
+        ),
+        in_specs=[vmem, vmem, anywhere, anywhere, vmem, vmem],
+        out_specs=(anywhere, anywhere, vmem, vmem),
+        scratch_shapes=[
+            pltpu.VMEM((model, hidden_units), half),
+            pltpu.VMEM((hidden_units, model), half),
+            pltpu.VMEM((model, hidden_units), half),
+            pltpu.VMEM((hidden_units, model), half),
+            pltpu.VMEM((2, 16, rows, width), half),
+            pltpu.VMEM((2, rows, width), half),
+            pltpu.VMEM((2, rows, width), half),
+            pltpu.VMEM((rows, hidden_units), full),
+            pltpu.VMEM((rows, hidden_units), full),
+            pltpu.VMEM((hidden_units, rows), half),
+            pltpu.VMEM((rows, hidden_units), half),
+            pltpu.VMEM((rows, 128), full),
+            pltpu.VMEM((16, rows, width), full),
+            pltpu.VMEM((8, rows, width), half),
+            pltpu.VMEM((8, rows, width), half),
+            pltpu.VMEM((4, rows, width), full),
+            pltpu.VMEM((4, rows, width), half),
+            pltpu.VMEM((4, rows, width), half),
+            pltpu.VMEM((3, rows, width), half),
+            pltpu.VMEM((3, rows, width), half),
+            pltpu.VMEM((rows, width), half),
+            pltpu.VMEM((rows, width), half),
+            pltpu.VMEM((3, 8, rows), full),
+            pltpu.VMEM((5, 8, rows), full),
+            pltpu.SemaphoreType.DMA((10,)),
+            pltpu.SemaphoreType.DMA((copies,)),
+            pltpu.SemaphoreType.DMA((copies,)),
+        ],
+        compiler_params=pltpu.CompilerParams(
+            collective_id=0, has_side_effects=True, vmem_limit_bytes=52 * 2**20
+        ),
+        cost_estimate=pl.CostEstimate(
+            flops=10 * rows * model * hidden_units,
+            bytes_accessed=8 * model * hidden_units,
+            transcendentals=rows * hidden_units,
+        ),
+    )(activations, out_grad, w_in, w_out, chosen, gate_scores)
+
+
+def fits(mesh, operands):
+    activations, _, w_in, _, chosen, _ = operands
+    return (
+        mesh.shape["dp"] == 16
+        and mesh.shape["expert"] == 2
+        and activations.shape[0] % 256 == 0
+        and activations.shape[1] == 4096
+        and w_in.shape == (2, 4096, 8192)
+        and chosen.shape == (2, 256)
+    )
+
 
 def solution(mesh):
-    return jax.shard_map(
-        per_device,
-        mesh=mesh,
-        in_specs=(
-            P("expert", "dp"),
-            P("expert", "dp"),
-            P("expert", None, "dp"),
-            P("expert", "dp", None),
-            P(),
-            P("expert", None),
-        ),
-        out_specs=(
-            P("expert", None, "dp"),
-            P("expert", "dp", None),
-            P("expert", "dp"),
-            P("expert", None),
-        ),
-        check_vma=False,
-    )
+    def run(*operands):
+        body = fused if fits(mesh, operands) else per_device
+        return jax.shard_map(
+            body,
+            mesh=mesh,
+            in_specs=(
+                P("expert", "dp"),
+                P("expert", "dp"),
+                P("expert", None, "dp"),
+                P("expert", "dp", None),
+                P(),
+                P("expert", None),
+            ),
+            out_specs=(
+                P("expert", None, "dp"),
+                P("expert", "dp", None),
+                P("expert", "dp"),
+                P("expert", None),
+            ),
+            check_vma=False,
+        )(*operands)
+
+    return run

time: 210 us -> 83.4 us (0.40)
  waiting for transfers between devices: 109 us -> 0 us
  Pallas kernels: 0 us -> 71.4 us
  blocking collectives: 58.3 us -> 0 us
  matrix products: 24.5 us -> 0 us
  between operations: 13.8 us -> 0.66 us
  local copies, waits for them, and re-layouts: 3.12 us -> 11.2 us
    all_gather x2 -> x0, waiting for transfers between devices: 80.5 us -> none  [the longest x1 41.7 us: per_device(): lax.all_gather(jnp.take(every_act, picked, axis=0), 'dp', axis=1, tiled=T...]
    pallas_call x0 -> x1, Pallas kernels: none -> 71.4 us  [fused(): pl.pallas_call(fused_kernel, out_shape=(jax.ShapeDtypeStruct((1, model, h...]
    psum x1 -> x0, blocking collectives: 32.5 us -> none  [per_device(): lax.psum(jnp.sum(hidden.astype(jnp.float32) * raw_back, axis=1), 'dp')]
    reduce_scatter x1 -> x0, waiting for transfers between devices: 27.9 us -> none  [input_sum(): lax.psum_scatter(contract(weight_in, preact_back, 1, 1), 'dp', scatter_di...]
    all_gather x3 -> x0, blocking collectives: 25.8 us -> none  [the longest x1 10.2 us: per_device(): lax.all_gather(activations, 'expert', axis=0, tiled=True)]
    dot_general x8 -> x0, matrix products: 24.5 us -> none  [the longest x5 18.9 us: contract(): lax.dot_general(left_operand, right_operand, (((left_axis,), (right_axis,...]
    unnamed x8 -> x14, local copies, waits for them, and re-layouts: 0.02 us -> 11.2 us
    gather x2 -> x0, local copies, waits for them, and re-layouts: 2.3 us -> none  [the longest x1 1.15 us: per_device(): jnp.take(every_act, picked, axis=0)]
  transfers between devices with their start and end apart: 3 -> 0, of which waited for: 3 -> 0; matrix products, arithmetic and copies ran while one was open for 7% -> 0% of each run, Pallas kernels for 0% -> 0%
where the time goes in v1:
time: 83.4 us; the launch traced here: 83.2 us
  Pallas kernels  71.4 us (86%)
  local copies, waits for them, and re-layouts  11.2 us (13%)
    pallas_call x1, Pallas kernels, fused(): pl.pallas_call(fused_kernel, out_shape=(jax.ShapeDtypeStruct((1, model, h...  71.4 us
    unnamed x14, local copies, waits for them, and re-layouts  11.2 us

profile of v1, /device:TPU:0, one launch (start us, length us, event | category | flops | bytes accessed | tf_op | source)
XLA Modules:
  0.0 83.2 jit_solution(9427828953034270866)
XLA Ops:
  0.6 0.0 copy-start
  0.6 0.9 %copy-done = bf16[512,256]{1,0:T(8,128)(2,1)S(1)} copy-done((bf16[512,256]{1,0:T(8,128)(2,1)S(1)}, bf16[512,256]{1,0:T(8,128)(2,1)}, u32[]{:S(2)}) %copy-start) | copy-done | bytes 262168
  1.6 0.0 copy-start.1
  1.6 0.9 %copy-done.1 = bf16[512,256]{1,0:T(8,128)(2,1)S(1)} copy-done((bf16[512,256]{1,0:T(8,128)(2,1)S(1)}, bf16[512,256]{1,0:T(8,128)(2,1)}, u32[]{:S(2)}) %copy-start.1) | copy-done | bytes 262168
  2.5 0.0 copy-start.2
  2.5 0.7 copy-done.2
  3.2 0.0 copy-start.3
  3.2 0.7 copy-done.3
  3.9 71.4 %shard_map.93 = (bf16[1,4096,512]{2,1,0:T(8,128)(2,1)}, bf16[1,512,4096]{2,1,0:T(8,128)(2,1)}, bf16[512,256]{1,0:T(8,128)(2,1)S(1)}, f32[1,256]{1,0:T(1,128)S(1)}) custom-call(bf16[512,256]{1,0:T(8,128)(2,1)S(1)} %copy-done, bf16[512,256]{1,0:T(8,128)(2,1)S(1)} %copy-done.1, bf16[1,4096,512]{2,1,0:T(8,128)(2,1)} %win_hbm.1, bf16[1,512,4096]{2,1,0:T(8,128)(2,1)} %wout_hbm.1, ...), custom_call_target="tpu_custom_call" | custom-call | flops 5368709120 | bytes 16777216 | tf_op jit(solution)/shard_map/pallas_call | solution.py:359
  75.3 0.0 copy-start.4
  75.3 4.6 %copy.14 = bf16[1,4096,512]{2,1,0:T(8,128)(2,1)} copy(bf16[1,4096,512]{2,1,0:T(8,128)(2,1)} %get-tuple-element.8) | data formatting | bytes 8388608
  79.9 0.0 copy-done.4
  79.9 2.0 %copy.15 = bf16[1,512,4096]{2,1,0:T(8,128)(2,1)} copy(bf16[1,512,4096]{2,1,0:T(8,128)(2,1)S(1)} %copy-done.4) | data formatting | bytes 8388608
  82.0 0.7 copy.16
  82.7 0.6 copy.17
Async XLA Ops:
  0.6 1.0 %copy-start = (bf16[512,256]{1,0:T(8,128)(2,1)S(1)}, bf16[512,256]{1,0:T(8,128)(2,1)}, u32[]{:S(2)}) copy-start(bf16[512,256]{1,0:T(8,128)(2,1)} %act_ref.1) | copy-start | bytes 786436
  1.6 0.9 %copy-start.1 = (bf16[512,256]{1,0:T(8,128)(2,1)S(1)}, bf16[512,256]{1,0:T(8,128)(2,1)}, u32[]{:S(2)}) copy-start(bf16[512,256]{1,0:T(8,128)(2,1)} %grad_ref.1) | copy-start | bytes 786436
  2.5 0.7 copy-start.2
  3.2 0.7 copy-start.3
  75.3 4.6 %copy-start.4 = (bf16[1,512,4096]{2,1,0:T(8,128)(2,1)S(1)}, bf16[1,512,4096]{2,1,0:T(8,128)(2,1)}, u32[]{:S(2)}) copy-start(bf16[1,512,4096]{2,1,0:T(8,128)(2,1)} %get-tuple-element.9) | copy-start | bytes 12582916

commit v2 on v1

--- a/solution.py
+++ b/solution.py
@@ -85,11 +85,11 @@
 
 
 def fused_kernel(
-    act_ref, grad_ref, win_hbm, wout_hbm, chosen_ref, scores_ref,
-    wing_hbm, woutg_hbm, actg_ref, gate_ref,
-    win_v, wout_v, wing_v, woutg_v, gat, xsend, xrecv, pre, raw,
+    act_hbm, grad_hbm, win_hbm, wout_hbm, chosen_hbm, scores_hbm,
+    wing_v, woutg_v, actg_ref, gate_ref,
+    act_ref, grad_ref, chosen_ref, scores_ref, win_v, wout_v, gat, xsend, xrecv, pre, raw,
     hidden_t, back_b, gate_rows, part, s_send, s_recv, q_keep, y_send, y_recv,
-    z_send, z_recv, t_send, t_recv, g_send, g_recv, local_sem, send_sem, recv_sem,
+    z_send, z_recv, t_send, t_recv, g_send, g_recv, local_sem, send_sem, recv_sem, gather_sem,
 ):
     me = lax.axis_index("dp")
     expert = lax.axis_index("expert")
@@ -99,7 +99,6 @@
     rows = chosen_ref.shape[1]
     hidden_units = win_v.shape[1]
     zgroups = 4
-    group_width = 4 * width
 
     def peer(mask):
         index = 0
@@ -111,19 +110,26 @@
     x_peer = {"expert": other}
 
     def group_of(kz):
-        low = 1 - bits[2] if kz & 1 else bits[2]
-        high = 1 - bits[3] if kz & 2 else bits[3]
-        return low + 2 * high
+        return flip(bits[2], kz % 2) + 2 * flip(bits[3], kz // 2)
 
     loads = [
-        pltpu.make_async_copy(win_hbm.at[0], win_v, local_sem.at[0]),
-        pltpu.make_async_copy(wout_hbm.at[0], wout_v, local_sem.at[1]),
+        pltpu.make_async_copy(source, landing, local_sem.at[number])
+        for number, (source, landing) in enumerate(
+            (
+                (chosen_hbm, chosen_ref),
+                (act_hbm, act_ref),
+                (grad_hbm, grad_ref),
+                (scores_hbm, scores_ref),
+                (win_hbm.at[0], win_v),
+                (wout_hbm.at[0], wout_v),
+            )
+        )
     ]
     for load in loads:
         load.start()
 
     barrier = pltpu.get_barrier_semaphore()
-    targets = [peer(1), peer(2), peer(4), peer(8), peer(12), x_peer]
+    targets = [x_peer, peer(1), peer(2), peer(4), peer(8), peer(12)]
     for target in targets:
         pl.semaphore_signal(
             barrier, inc=1, device_id=target, device_id_type=pl.DeviceIdType.MESH
@@ -135,8 +141,9 @@
         picked = chosen_ref[pl.ds(which, 1), :]
         return jnp.where(picked == token, 1.0, 0.0).astype(jnp.bfloat16)
 
+    loads[0].wait()
+    other_hot = onehot(other)
     own_hot = onehot(expert)
-    other_hot = onehot(other)
 
     ids = {}
 
@@ -160,9 +167,11 @@
         started.append(copy)
         incoming[key] = copy
 
+    loads[1].wait()
     xsend[0] = contract(other_hot, act_ref[...], 0, 0).astype(jnp.bfloat16)
     pl.semaphore_wait(barrier, len(targets))
     send(xsend.at[0], xrecv.at[0], x_peer, ("x", 0))
+    loads[2].wait()
     xsend[1] = contract(other_hot, grad_ref[...], 0, 0).astype(jnp.bfloat16)
     send(xsend.at[1], xrecv.at[1], x_peer, ("x", 1))
     own_picks = [
@@ -172,11 +181,51 @@
     pre[...] = jnp.zeros_like(pre)
     raw[...] = jnp.zeros_like(raw)
 
-    def pass_on(array, k, mask):
-        send(gat.at[array, k], gat.at[array, k ^ mask], peer(mask), ("g", array, k ^ mask))
-
-    def arrived(array, k):
-        incoming[("g", array, k)].wait_recv()
+    inner = flip(bits[2], bits[3])
+    by_inner = []
+
+    def pass_on(array, slot, landing, target, key):
+        copy = pltpu.make_async_remote_copy(
+            src_ref=gat.at[array, slot],
+            dst_ref=gat.at[array, landing],
+            send_sem=send_sem.at[slot_of(("g", array) + key)],
+            recv_sem=gather_sem.at[array, landing],
+            device_id=target,
+            device_id_type=pl.DeviceIdType.MESH,
+        )
+        return copy
+
+    def begin(copy):
+        copy.start()
+        started.append(copy)
+
+    def arrived(array, slot):
+        pltpu.make_async_remote_copy(
+            src_ref=gat.at[array, slot],
+            dst_ref=gat.at[array, slot],
+            send_sem=send_sem.at[0],
+            recv_sem=gather_sem.at[array, slot],
+            device_id=peer(1),
+            device_id_type=pl.DeviceIdType.MESH,
+        ).wait_recv()
+
+    def to_pair(array, kz, low, step):
+        begin(
+            pass_on(array, 4 * kz + low, 4 * kz + low + 1, peer(1), ("pair", step, low))
+        )
+
+    def to_column(array, kz, step):
+        begin(
+            pass_on(array, 4 * kz, 4 * kz + 2, peer(2), ("column", step))
+        )
+
+    def along_line(array, slot, landing, mask, step):
+        copy = pass_on(array, slot, landing, peer(mask), ("line", step))
+        by_inner.append(copy)
+
+        @pl.when(inner == 1)
+        def _():
+            copy.start()
 
     def add_group(kz):
         base = group_of(kz)
@@ -194,28 +243,40 @@
 
         lax.fori_loop(0, 4, body, 0)
 
+    kz_at = [0, 1, 2 + inner, 3 - inner]
     for array in range(2):
         incoming[("x", array)].wait_recv()
         gat[array, 0] = own_picks[array] + xrecv[array]
-        for mask in (4, 2, 8, 12, 1):
-            pass_on(array, 0, mask)
-    for load in loads:
+        begin(pass_on(array, 0, 4, peer(4), ("own",)))
+        along_line(array, 0, 12, 12, 0)
+        to_column(array, 0, 0)
+        to_pair(array, 0, 0, 0)
+    for load in loads[3:]:
         load.wait()
     for step in range(1, zgroups + 2):
         for array in range(2):
             if step < zgroups:
-                arrived(array, 4 * step)
-                pass_on(array, 4 * step, 2)
-                pass_on(array, 4 * step, 1)
+                kz = kz_at[step]
+                arrived(array, 4 * kz)
+                if step == 1:
+                    along_line(array, 4, 8, 12, 1)
+                elif step == 2:
+                    along_line(array, 12, 8, 4, 2)
+                else:
+                    along_line(array, 8, 12, 4, 3)
+                to_column(array, kz, step)
+                to_pair(array, kz, 0, step)
         for array in range(2):
             if step <= zgroups:
-                arrived(array, 4 * (step - 1) + 2)
-                pass_on(array, 4 * (step - 1) + 2, 1)
+                kz = kz_at[step - 1]
+                arrived(array, 4 * kz + 2)
+                to_pair(array, kz, 2, step - 1)
         if step >= 2:
+            kz = kz_at[step - 2]
             for array in range(2):
-                arrived(array, 4 * (step - 2) + 1)
-                arrived(array, 4 * (step - 2) + 3)
-            add_group(step - 2)
+                arrived(array, 4 * kz + 1)
+                arrived(array, 4 * kz + 3)
+            add_group(kz)
 
     chunk = 32
     score_col = jnp.broadcast_to(scores_ref[...], (128, rows)).T
@@ -278,8 +339,6 @@
     send(g_send.at[0], g_recv.at[0], peer(1), ("gate", 0))
     hidden_t[...] = pre[...].T.astype(jnp.bfloat16)
 
-    stores = []
-
     def weight_grads(kz):
         base = group_of(kz)
 
@@ -296,17 +355,6 @@
             return carry
 
         lax.fori_loop(0, 4, body, 0)
-        span = pl.ds(pl.multiple_of(base * group_width, group_width), group_width)
-        for copy in (
-            pltpu.make_async_copy(
-                wing_v.at[span, :], wing_hbm.at[0, span, :], local_sem.at[2 + 2 * kz]
-            ),
-            pltpu.make_async_copy(
-                woutg_v.at[:, span], woutg_hbm.at[0, :, span], local_sem.at[3 + 2 * kz]
-            ),
-        ):
-            copy.start()
-            stores.append(copy)
 
     weight_grads(0)
     incoming[("gate", 0)].wait_recv()
@@ -342,10 +390,34 @@
     incoming[("t", 0)].wait_recv()
     theirs = jnp.dot(other_hot, t_recv[...], preferred_element_type=jnp.float32)
     actg_ref[...] = (mine + theirs).astype(jnp.bfloat16)
-    for copy in stores:
-        copy.wait()
     for copy in started:
         copy.wait_send()
+
+    @pl.when(inner == 1)
+    def _():
+        for copy in by_inner:
+            copy.wait_send()
+
+
+def store_kernel(*refs):
+    sources, results, sems = refs[:4], refs[4:8], refs[8]
+    pieces = 4
+    copies = []
+    for place in range(2):
+        source, result = sources[place], results[place].at[0]
+        step = source.shape[0] // pieces
+        for piece in range(pieces):
+            span = pl.ds(piece * step, step)
+            copies.append((source.at[span], result.at[span]))
+    copies += [(sources[place], results[place]) for place in (2, 3)]
+    running = [
+        pltpu.make_async_copy(source, result, sems.at[number])
+        for number, (source, result) in enumerate(copies)
+    ]
+    for copy in running:
+        copy.start()
+    for copy in running:
+        copy.wait()
 
 
 def fused(activations, out_grad, w_in, w_out, chosen, gate_scores):
@@ -355,20 +427,22 @@
     copies = 64
     half, full = jnp.bfloat16, jnp.float32
     vmem = pl.BlockSpec(memory_space=pltpu.VMEM)
-    anywhere = pl.BlockSpec(memory_space=pl.ANY)
-    return pl.pallas_call(
+    in_hbm = pl.BlockSpec(memory_space=pltpu.HBM)
+    results = pl.pallas_call(
         fused_kernel,
         out_shape=(
-            jax.ShapeDtypeStruct((1, model, hidden_units), half),
-            jax.ShapeDtypeStruct((1, hidden_units, model), half),
+            jax.ShapeDtypeStruct((model, hidden_units), half),
+            jax.ShapeDtypeStruct((hidden_units, model), half),
             jax.ShapeDtypeStruct((own_rows, width), half),
             jax.ShapeDtypeStruct((1, rows), full),
         ),
-        in_specs=[vmem, vmem, anywhere, anywhere, vmem, vmem],
-        out_specs=(anywhere, anywhere, vmem, vmem),
+        in_specs=[in_hbm] * 6,
+        out_specs=(vmem,) * 4,
         scratch_shapes=[
-            pltpu.VMEM((model, hidden_units), half),
-            pltpu.VMEM((hidden_units, model), half),
+            pltpu.VMEM((own_rows, width), half),
+            pltpu.VMEM((own_rows, width), half),
+            pltpu.VMEM(chosen.shape, chosen.dtype),
+            pltpu.VMEM((1, rows), full),
             pltpu.VMEM((model, hidden_units), half),
             pltpu.VMEM((hidden_units, model), half),
             pltpu.VMEM((2, 16, rows, width), half),
@@ -394,9 +468,10 @@
             pltpu.SemaphoreType.DMA((10,)),
             pltpu.SemaphoreType.DMA((copies,)),
             pltpu.SemaphoreType.DMA((copies,)),
+            pltpu.SemaphoreType.DMA((2, 16)),
         ],
         compiler_params=pltpu.CompilerParams(
-            collective_id=0, has_side_effects=True, vmem_limit_bytes=52 * 2**20
+            collective_id=0, has_side_effects=True, vmem_limit_bytes=44 * 2**20
         ),
         cost_estimate=pl.CostEstimate(
             flops=10 * rows * model * hidden_units,
@@ -404,6 +479,18 @@
             transcendentals=rows * hidden_units,
         ),
     )(activations, out_grad, w_in, w_out, chosen, gate_scores)
+    return pl.pallas_call(
+        store_kernel,
+        out_shape=(
+            jax.ShapeDtypeStruct((1, model, hidden_units), half),
+            jax.ShapeDtypeStruct((1, hidden_units, model), half),
+            jax.ShapeDtypeStruct((own_rows, width), half),
+            jax.ShapeDtypeStruct((1, rows), full),
+        ),
+        in_specs=[vmem] * 4,
+        out_specs=(in_hbm,) * 4,
+        scratch_shapes=[pltpu.SemaphoreType.DMA((10,))],
+    )(*results)
 
 
 def fits(mesh, operands):

time: 83.4 us -> 84.9 us (1.018)
  Pallas kernels: 71.4 us -> 75.6 us
  local copies, waits for them, and re-layouts: 11.2 us -> 8.4 us
    pallas_call x1 -> x2, Pallas kernels: 71.4 us -> 75.6 us  [the longest x1 68.7 us: fused(): pl.pallas_call(fused_kernel, out_shape=(jax.ShapeDtypeStruct((model, hidd...]
    unnamed x14 -> x16, local copies, waits for them, and re-layouts: 11.2 us -> 8.4 us
where the time goes in v2:
time: 84.9 us; the launch traced here: 84.7 us
  Pallas kernels  75.6 us (89%)
  local copies, waits for them, and re-layouts  8.4 us (10%)
    pallas_call x1, Pallas kernels, fused(): pl.pallas_call(fused_kernel, out_shape=(jax.ShapeDtypeStruct((model, hidd...  68.7 us
    unnamed x16, local copies, waits for them, and re-layouts  8.4 us
    pallas_call x1, Pallas kernels, fused(): pl.pallas_call(store_kernel, out_shape=(jax.ShapeDtypeStruct((1, model, h...  6.9 us

profile of v2, /device:TPU:0, one launch (start us, length us, event | category | flops | bytes accessed | tf_op | source)
XLA Modules:
  0.0 84.7 jit_solution(16919238089380631547)
XLA Ops:
  0.6 0.0 copy-start.4
  0.6 0.9 %copy-done.4 = bf16[512,256]{1,0:T(8,128)(2,1)S(1)} copy-done((bf16[512,256]{1,0:T(8,128)(2,1)S(1)}, bf16[512,256]{1,0:T(8,128)(2,1)}, u32[]{:S(2)}) %copy-start.4) | copy-done | bytes 262168
  1.6 0.0 copy-start.5
  1.6 0.9 %copy-done.5 = bf16[512,256]{1,0:T(8,128)(2,1)S(1)} copy-done((bf16[512,256]{1,0:T(8,128)(2,1)S(1)}, bf16[512,256]{1,0:T(8,128)(2,1)}, u32[]{:S(2)}) %copy-start.5) | copy-done | bytes 262168
  2.5 0.0 copy-start.6
  2.5 0.7 copy-done.6
  3.2 0.0 copy-start.7
  3.2 0.7 copy-done.7
  3.9 68.7 %shard_map.93 = (bf16[4096,512]{1,0:T(8,128)(2,1)S(1)}, bf16[512,4096]{1,0:T(8,128)(2,1)S(1)}, bf16[512,256]{1,0:T(8,128)(2,1)S(1)}, f32[1,256]{1,0:T(1,128)S(1)}) custom-call(bf16[512,256]{1,0:T(8,128)(2,1)S(1)} %copy-done.4, bf16[512,256]{1,0:T(8,128)(2,1)S(1)} %copy-done.5, bf16[1,4096,512]{2,1,0:T(8,128)(2,1)} %win_hbm.1, ...), custom_call_target="tpu_custom_call" | custom-call | flops 5368709120 | bytes 16777216 | tf_op jit(solution)/shard_map/pallas_call | solution.py:431
  72.7 0.0 copy-start
  72.7 1.9 %copy-done = bf16[4096,512]{1,0:T(8,128)(2,1)} copy-done((bf16[4096,512]{1,0:T(8,128)(2,1)}, bf16[4096,512]{1,0:T(8,128)(2,1)S(1)}, u32[]{:S(2)}) %copy-start) | copy-done | bytes 4194328
  74.6 0.0 copy-start.1
  74.6 2.0 %copy-done.1 = bf16[512,4096]{1,0:T(8,128)(2,1)} copy-done((bf16[512,4096]{1,0:T(8,128)(2,1)}, bf16[512,4096]{1,0:T(8,128)(2,1)S(1)}, u32[]{:S(2)}) %copy-start.1) | copy-done | bytes 4194328
  76.6 0.0 copy-start.2
  76.6 0.7 copy-done.2
  77.3 0.0 copy-start.3
  77.3 0.5 copy-done.3
  77.8 6.9 %shard_map.94 = (bf16[1,4096,512]{2,1,0:T(8,128)(2,1)}, bf16[1,512,4096]{2,1,0:T(8,128)(2,1)}, bf16[512,256]{1,0:T(8,128)(2,1)}, f32[1,256]{1,0:T(1,128)}) custom-call(bf16[4096,512]{1,0:T(8,128)(2,1)} %copy-done, bf16[512,4096]{1,0:T(8,128)(2,1)} %copy-done.1, bf16[512,256]{1,0:T(8,128)(2,1)} %copy-done.2, f32[1,256]{1,0:T(1,128)} %copy-done.3), custom_call_target="tpu_custom_call" | custom-call | tf_op jit(solution)/shard_map/pallas_call | solution.py:482
Async XLA Ops:
  0.6 1.0 %copy-start.4 = (bf16[512,256]{1,0:T(8,128)(2,1)S(1)}, bf16[512,256]{1,0:T(8,128)(2,1)}, u32[]{:S(2)}) copy-start(bf16[512,256]{1,0:T(8,128)(2,1)} %act_hbm.1) | copy-start | bytes 786436
  1.6 0.9 %copy-start.5 = (bf16[512,256]{1,0:T(8,128)(2,1)S(1)}, bf16[512,256]{1,0:T(8,128)(2,1)}, u32[]{:S(2)}) copy-start(bf16[512,256]{1,0:T(8,128)(2,1)} %grad_hbm.1) | copy-start | bytes 786436
  2.5 0.7 copy-start.6
  3.2 0.7 copy-start.7
  72.7 1.9 %copy-start = (bf16[4096,512]{1,0:T(8,128)(2,1)}, bf16[4096,512]{1,0:T(8,128)(2,1)S(1)}, u32[]{:S(2)}) copy-start(bf16[4096,512]{1,0:T(8,128)(2,1)S(1)} %get-tuple-element.8.refs_0_) | copy-start | bytes 12582916
  74.6 2.0 %copy-start.1 = (bf16[512,4096]{1,0:T(8,128)(2,1)}, bf16[512,4096]{1,0:T(8,128)(2,1)S(1)}, u32[]{:S(2)}) copy-start(bf16[512,4096]{1,0:T(8,128)(2,1)S(1)} %get-tuple-element.9.refs_1_) | copy-start | bytes 12582916
  76.6 0.7 copy-start.2
  77.3 0.5 copy-start.3

commit v3 on v2

--- a/solution.py
+++ b/solution.py
@@ -490,6 +490,7 @@
         in_specs=[vmem] * 4,
         out_specs=(in_hbm,) * 4,
         scratch_shapes=[pltpu.SemaphoreType.DMA((10,))],
+        compiler_params=pltpu.CompilerParams(vmem_limit_bytes=2**20),
     )(*results)
 
 

time: 84.9 us -> 76.3 us (0.90)
  local copies, waits for them, and re-layouts: 8.4 us -> 3.25 us
  Pallas kernels: 75.6 us -> 72.2 us
    unnamed x16 -> x8, local copies, waits for them, and re-layouts: 8.4 us -> 3.25 us
    pallas_call x1, Pallas kernels: 6.9 us -> 3.44 us  [fused(): pl.pallas_call(store_kernel, out_shape=(jax.ShapeDtypeStruct((1, model, h...]
where the time goes in v3:
time: 76.3 us; the launch traced here: 76.1 us
  Pallas kernels  72.2 us (95%)
  local copies, waits for them, and re-layouts  3.25 us (4%)
    pallas_call x1, Pallas kernels, fused(): pl.pallas_call(fused_kernel, out_shape=(jax.ShapeDtypeStruct((model, hidd...  68.7 us
    pallas_call x1, Pallas kernels, fused(): pl.pallas_call(store_kernel, out_shape=(jax.ShapeDtypeStruct((1, model, h...  3.44 us
    unnamed x8, local copies, waits for them, and re-layouts  3.25 us

profile of v3, /device:TPU:0, one launch (start us, length us, event | category | flops | bytes accessed | tf_op | source)
XLA Modules:
  0.0 76.1 jit_solution(1537050517505461408)
XLA Ops:
  0.6 0.0 copy-start
  0.6 0.9 %copy-done = bf16[512,256]{1,0:T(8,128)(2,1)S(1)} copy-done((bf16[512,256]{1,0:T(8,128)(2,1)S(1)}, bf16[512,256]{1,0:T(8,128)(2,1)}, u32[]{:S(2)}) %copy-start) | copy-done | bytes 262168
  1.6 0.0 copy-start.1
  1.6 0.9 %copy-done.1 = bf16[512,256]{1,0:T(8,128)(2,1)S(1)} copy-done((bf16[512,256]{1,0:T(8,128)(2,1)S(1)}, bf16[512,256]{1,0:T(8,128)(2,1)}, u32[]{:S(2)}) %copy-start.1) | copy-done | bytes 262168
  2.5 0.0 copy-start.2
  2.5 0.7 copy-done.2
  3.2 0.0 copy-start.3
  3.2 0.7 copy-done.3
  3.9 68.7 %shard_map.93 = (bf16[4096,512]{1,0:T(8,128)(2,1)S(1)}, bf16[512,4096]{1,0:T(8,128)(2,1)S(1)}, bf16[512,256]{1,0:T(8,128)(2,1)S(1)}, f32[1,256]{1,0:T(1,128)S(1)}) custom-call(bf16[512,256]{1,0:T(8,128)(2,1)S(1)} %copy-done, bf16[512,256]{1,0:T(8,128)(2,1)S(1)} %copy-done.1, bf16[1,4096,512]{2,1,0:T(8,128)(2,1)} %win_hbm.1, bf16[1,512,4096]{2,1,0:T(8,128)(2,1)} %wout_hbm.1, ...), custom_call_target="tpu_custom_call" | custom-call | flops 5368709120 | bytes 16777216 | tf_op jit(solution)/shard_map/pallas_call | solution.py:431
  72.7 3.4 %shard_map.94 = (bf16[1,4096,512]{2,1,0:T(8,128)(2,1)}, bf16[1,512,4096]{2,1,0:T(8,128)(2,1)}, bf16[512,256]{1,0:T(8,128)(2,1)}, f32[1,256]{1,0:T(1,128)}) custom-call(bf16[4096,512]{1,0:T(8,128)(2,1)S(1)} %get-tuple-element.8.refs_0_, bf16[512,4096]{1,0:T(8,128)(2,1)S(1)} %get-tuple-element.9.refs_1_, bf16[512,256]{1,0:T(8,128)(2,1)S(1)} %get-tuple-element.10.refs_2_, ...), custom_call_target="tpu_custom_call" | custom-call | tf_op jit(solution)/shard_map/pallas_call | solution.py:482
Async XLA Ops:
  0.6 1.0 %copy-start = (bf16[512,256]{1,0:T(8,128)(2,1)S(1)}, bf16[512,256]{1,0:T(8,128)(2,1)}, u32[]{:S(2)}) copy-start(bf16[512,256]{1,0:T(8,128)(2,1)} %act_hbm.1) | copy-start | bytes 786436
  1.6 0.9 %copy-start.1 = (bf16[512,256]{1,0:T(8,128)(2,1)S(1)}, bf16[512,256]{1,0:T(8,128)(2,1)}, u32[]{:S(2)}) copy-start(bf16[512,256]{1,0:T(8,128)(2,1)} %grad_hbm.1) | copy-start | bytes 786436
  2.5 0.7 copy-start.2
  3.2 0.7 copy-start.3
